TPU v7x, 256 devices: a whole 4x4x8 slice. The times are simulated.
256 devices in a mesh: src: 16 (over z, x_hi), tgt: 16 (over x_lo, y, core).
Axes of the slice: x: 4 (x_hi: 2, x_lo: 2; x = x_hi * 2 + x_lo), y: 4, z: 8, core: 2. Of those that a mesh axis runs over, the one named last changes fastest.
Arguments:
- src_emb: bfloat16 [64, 32768], P(None, 'src'), may hold values from -2.75 to 2.75
- tgt_emb: bfloat16 [64, 131072], P(None, 'tgt'), may hold values from -2.75 to 2.75
- target_features: bfloat16 [128, 131072], P(None, 'tgt'), may hold values from -6 to 6
- src_mass: float32 [32768], P('src'), may hold values from 1 to 10
- tgt_mass: float32 [131072], P('tgt'), may hold values from 1 to 10
- kept_blocks: int32 [128, 128], P('src', 'tgt'), may hold values from 0 to 31, as said below
- kept_count: int32 [128, 16], P('src', 'tgt'), may hold values from 1 to 8
Outputs:
- projected: float32 [32768, 128], P(('src', 'tgt'))
- src_potential: float32 [32768], P('src')
- tgt_potential: float32 [131072], P('tgt')
Inputs may be any that keep to these rules, and one draw needn't show every extreme that they name: `kept_blocks`: entry [r, t * 8 + k] is a block number within target shard t; the 8 entries of one group are distinct; the first kept_count[r, t] of them are kept, the others are unused; every target block is kept by some source block row.
All inputs are finite; a program needn't handle non-finite values.
Results may differ from a plain program's by a relative error of at most 0.00075.
Values sent between devices are 32-bit elements; how exact they have to be, the bound alone decides.
A program may use at most 64 MiB of HBM per device.

v0:
```python
import jax
import jax.numpy as jnp
from jax import lax
from jax.sharding import PartitionSpec as P

BLOCK = 256
ITERS = 2
SENTINEL = -1e30
EPSILON = 0.1


def pair_distance(src_tile, norm_tile, tgt_chosen, tgt_norm_chosen):
    products = jnp.einsum("dr,dkc->krc", src_tile, tgt_chosen, preferred_element_type=jnp.float32)
    return norm_tile[None, :, None] + tgt_norm_chosen[:, None, :] - 2.0 * products


def merge_rows(highest, totals):
    overall = lax.pmax(highest, "tgt")
    return (overall, lax.psum(totals * jnp.exp(highest - overall), "tgt"))


def merge_columns(block_top, block_sum):
    overall = lax.pmax(block_top, "src")
    return (overall, lax.psum(block_sum * jnp.exp(block_top - overall), "src"))


def shards(src_emb, tgt_emb, target_features, src_mass, tgt_mass, kept_blocks, kept_count):
    emb_width = src_emb.shape[0]
    src_rows = src_emb.shape[1]
    tgt_rows = tgt_emb.shape[1]
    src_blocks = src_rows // BLOCK
    tgt_blocks = tgt_rows // BLOCK
    slot_count = kept_blocks.shape[1]
    src_tiles = src_emb.reshape(emb_width, src_blocks, BLOCK).transpose(1, 0, 2)
    src_norm = jnp.sum(jnp.square(src_emb.astype(jnp.float32)), axis=0).reshape(src_blocks, BLOCK)
    tgt_tiles = tgt_emb.reshape(emb_width, tgt_blocks, BLOCK)
    target_norm = jnp.sum(jnp.square(tgt_emb.astype(jnp.float32)), axis=0).reshape(
        tgt_blocks, BLOCK
    )
    feat_tiles = target_features.reshape(target_features.shape[0], tgt_blocks, BLOCK)
    live_slot = lax.broadcasted_iota(jnp.int32, (src_blocks, slot_count), 1) < kept_count
    packets = (src_tiles, src_norm, kept_blocks, live_slot)
    flat_index = kept_blocks.reshape(-1)
    member = (
        lax.broadcasted_iota(jnp.int32, (tgt_blocks, flat_index.shape[0]), 0) == flat_index[None, :]
    )

    def distances(packet):
        return pair_distance(
            packet[0],
            packet[1],
            jnp.take(tgt_tiles, packet[2], axis=1),
            jnp.take(target_norm, packet[2], axis=0),
        )

    def row_scaled(potential_tiles, packet):
        scaled = (
            jnp.take(potential_tiles, packet[2], axis=0)[:, None, :] - distances(packet)
        ) / EPSILON
        return jnp.where(packet[3][:, None, None], scaled, SENTINEL)

    tgt_potential = jnp.zeros((tgt_rows,), jnp.float32)
    src_potential = jnp.zeros((src_rows,), jnp.float32)
    for iteration in range(ITERS):
        row_potential_tiles = tgt_potential.reshape(tgt_blocks, BLOCK)

        def row_per_block(packet):
            scaled = row_scaled(row_potential_tiles, packet)
            highest = jnp.max(scaled, axis=(0, 2))
            totals = jnp.sum(
                jnp.where(packet[3][:, None, None], jnp.exp(scaled - highest[None, :, None]), 0.0),
                axis=(0, 2),
            )
            return (highest, totals)

        highest, totals = lax.map(row_per_block, packets)
        highest, totals = merge_rows(*(highest.reshape(src_rows), totals.reshape(src_rows)))
        src_potential = EPSILON * jnp.log(src_mass) - EPSILON * (highest + jnp.log(totals))
        column_potential_tiles = src_potential.reshape(src_blocks, BLOCK)

        def column_per_block(packet):
            scaled = (packet[4][None, :, None] - distances(packet)) / EPSILON
            scaled = jnp.where(packet[3][:, None, None], scaled, SENTINEL)
            highest = jnp.max(scaled, axis=1)
            totals = jnp.sum(
                jnp.where(packet[3][:, None, None], jnp.exp(scaled - highest[:, None, :]), 0.0),
                axis=1,
            )
            return (highest, totals)

        slot_top, slot_sum = lax.map(column_per_block, packets + (column_potential_tiles,))
        slot_top = slot_top.reshape(src_blocks * slot_count, BLOCK)
        slot_sum = slot_sum.reshape(src_blocks * slot_count, BLOCK)
        block_top = jnp.max(jnp.where(member[:, :, None], slot_top[None, :, :], SENTINEL), axis=1)
        scaled_sum = slot_sum * jnp.exp(slot_top - jnp.take(block_top, flat_index, axis=0))
        block_sum = jnp.dot(member.astype(jnp.float32), scaled_sum, precision=lax.Precision.HIGHEST)
        block_top, block_sum = merge_columns(
            *(block_top.reshape(tgt_rows), block_sum.reshape(tgt_rows))
        )
        tgt_potential = EPSILON * jnp.log(tgt_mass) - EPSILON * (block_top + jnp.log(block_sum))
    final_tiles = tgt_potential.reshape(tgt_blocks, BLOCK)

    def local_peak(packet):
        return jnp.max(row_scaled(final_tiles, packet), axis=(0, 2))

    local_top = lax.map(local_peak, packets)

    def weigh(packet):
        scaled = row_scaled(final_tiles, packet)
        weights = jnp.where(
            packet[3][:, None, None], jnp.exp(scaled - packet[4][None, :, None]), 0.0
        )
        rounded_count = lax.optimization_barrier(weights.astype(jnp.bfloat16))
        numerator = jnp.einsum(
            "krc,fkc->rf",
            rounded_count,
            jnp.take(feat_tiles, packet[2], axis=1),
            preferred_element_type=jnp.float32,
        )
        return (numerator, jnp.sum(rounded_count.astype(jnp.float32), axis=(0, 2)))

    numerator, denominator = lax.map(weigh, packets + (local_top,))
    numerator = numerator.reshape(src_rows, target_features.shape[0])
    denominator = denominator.reshape(src_rows)
    local_top = local_top.reshape(src_rows)
    share_rows = src_rows // lax.axis_size("tgt")
    first_row = lax.axis_index("tgt") * share_rows
    overall = lax.pmax(local_top, "tgt")
    factor = jnp.exp(local_top - overall)
    numerator = numerator * factor[:, None]
    denominator = denominator * factor
    numerator, denominator = lax.psum((numerator, denominator), "tgt")
    numerator = lax.dynamic_slice_in_dim(numerator, first_row, share_rows, 0)
    denominator = lax.dynamic_slice_in_dim(denominator, first_row, share_rows, 0)
    projected = numerator / denominator[:, None]
    return (projected, src_potential, tgt_potential)


def solution(mesh):
    return jax.shard_map(
        shards,
        mesh=mesh,
        in_specs=(
            P(None, "src"),
            P(None, "tgt"),
            P(None, "tgt"),
            P("src"),
            P("tgt"),
            P("src", "tgt"),
            P("src", "tgt"),
        ),
        out_specs=(P(("src", "tgt"), None), P("src"), P("tgt")),
        check_vma=False,
    )
```

profile of v0, /device:TPU:1, one launch (start us, length us, event | category | flops | bytes accessed | tf_op | source)
XLA Modules:
  0.0 761.6 jit_solution(7564907167131679846)
XLA Ops:
  11.3 26.2 %while.70 = (s32[]{:T(128)}, f32[8,256]{1,0:T(8,128)S(1)}, f32[8,256]{1,0:T(8,128)S(1)}, pred[8,8]{1,0:T(8,128)(4,1)S(1)}, s32[8,8]{1,0:T(8,128)S(1)}, /*index=5...) while((s32[]{:T(128)}, f32[8,256]{1,0:T(8,128)S(1)}, ...), condition=%wide.region_5.8_spmd, body=%wide.region_2.7_spmd.sunk | while | flops 72487472 | bytes 5143929 | solution.py:76
  37.5 30.2 %pmax.35 = f32[2048]{0:T(1024)S(1)} all-reduce(f32[2048]{0:T(1024)S(1)} %bitcast.348), channel_id=1, replica_groups=mesh['src'=16,'tgt'=16] {'tgt'}, use_global_device_ids=true, to_apply=%region_6.9 | all-reduce | flops 2048 | bytes 16384 | tf_op jit(solution)/shard_map/pmax | solution.py:18
  67.8 29.3 %psum.42 = f32[2048]{0:T(1024)S(1)} all-reduce(f32[2048]{0:T(1024)S(1)} %exponential_multiply_fusion.3), channel_id=1, replica_groups=mesh['src'=16,'tgt'=16] {'tgt'}, use_global_device_ids=true, to_apply=%region_7.10 | all-reduce | flops 2048 | bytes 16384 | tf_op jit(solution)/shard_map/psum | solution.py:19
  97.1 19.6 %while.71 = (s32[]{:T(128)}, f32[8,8,256]{2,1,0:T(8,128)S(1)}, f32[8,8,256]{2,1,0:T(8,128)S(1)}, pred[8,8]{1,0:T(8,128)(4,1)S(1)}, f32[8,256]{1,0:T(8,128)S(1)},...) while((s32[]{:T(128)}, f32[8,8,256]{2,1,0:T(8,128)S(1)}, ...), condition=%wide.region_11.14_spmd, body=%wide.region_8.13_spmd.sunk | while | flops 72481840 | bytes 5123405 | solution.py:91
  118.2 66.0 %pmax.36 = f32[8192]{0:T(1024)S(1)} all-reduce(f32[8192]{0:T(1024)S(1)} %bitcast.335), channel_id=1, replica_groups=mesh['src'=16,'tgt'=16] {'src'}, use_global_device_ids=true, to_apply=%region_13.16 | all-reduce | flops 8192 | bytes 65536 | tf_op jit(solution)/shard_map/pmax | solution.py:23
  184.3 58.0 %psum.43 = f32[8192]{0:T(1024)S(1)} all-reduce(f32[8192]{0:T(1024)S(1)} %exponential_multiply_fusion.1), channel_id=1, replica_groups=mesh['src'=16,'tgt'=16] {'src'}, use_global_device_ids=true, to_apply=%region_14.18 | all-reduce | flops 8192 | bytes 65536 | tf_op jit(solution)/shard_map/psum | solution.py:24
  242.3 26.1 %while.72 = (s32[]{:T(128)}, f32[8,256]{1,0:T(8,128)S(1)}, f32[8,256]{1,0:T(8,128)S(1)}, pred[8,8]{1,0:T(8,128)(4,1)S(1)}, s32[8,8]{1,0:T(8,128)S(1)}, /*index=5...) while((s32[]{:T(128)}, f32[8,256]{1,0:T(8,128)S(1)}, ...), condition=%wide.region_18.22_spmd, body=%wide.region_15.21_spmd.sunk | while | flops 72487472 | bytes 5111157 | solution.py:76
  268.5 55.3 %pmax.37 = f32[2048]{0:T(1024)S(1)} all-reduce(f32[2048]{0:T(1024)S(1)} %bitcast.350), channel_id=1, replica_groups=mesh['src'=16,'tgt'=16] {'tgt'}, use_global_device_ids=true, to_apply=%region_19.23 | all-reduce | flops 2048 | bytes 16384 | tf_op jit(solution)/shard_map/pmax | solution.py:18
  323.8 27.6 %psum.44 = f32[2048]{0:T(1024)S(1)} all-reduce(f32[2048]{0:T(1024)S(1)} %exponential_multiply_fusion.2), channel_id=1, replica_groups=mesh['src'=16,'tgt'=16] {'tgt'}, use_global_device_ids=true, to_apply=%region_20.24 | all-reduce | flops 2048 | bytes 16384 | tf_op jit(solution)/shard_map/psum | solution.py:19
  352.1 19.6 %while.73 = (s32[]{:T(128)}, f32[8,8,256]{2,1,0:T(8,128)S(1)}, f32[8,8,256]{2,1,0:T(8,128)S(1)}, pred[8,8]{1,0:T(8,128)(4,1)S(1)}, f32[8,256]{1,0:T(8,128)S(1)},...) while((s32[]{:T(128)}, f32[8,8,256]{2,1,0:T(8,128)S(1)}, ...), condition=%wide.region_24.28_spmd, body=%wide.region_21.27_spmd.sunk | while | flops 72481840 | bytes 5123405 | solution.py:91
  373.1 59.6 %pmax.38 = f32[8192]{0:T(1024)S(1)} all-reduce(f32[8192]{0:T(1024)S(1)} %bitcast.337), channel_id=1, replica_groups=mesh['src'=16,'tgt'=16] {'src'}, use_global_device_ids=true, to_apply=%region_26.30 | all-reduce | flops 8192 | bytes 65536 | tf_op jit(solution)/shard_map/pmax | solution.py:23
  432.8 58.6 %psum.45 = f32[8192]{0:T(1024)S(1)} all-reduce(f32[8192]{0:T(1024)S(1)} %exponential_multiply_fusion), channel_id=1, replica_groups=mesh['src'=16,'tgt'=16] {'src'}, use_global_device_ids=true, to_apply=%region_27.31 | all-reduce | flops 8192 | bytes 65536 | tf_op jit(solution)/shard_map/psum | solution.py:24
  492.0 24.2 %while.74 = (s32[]{:T(128)}, f32[8,256]{1,0:T(8,128)S(1)}, pred[8,8]{1,0:T(8,128)(4,1)S(1)}, s32[8,8]{1,0:T(8,128)S(1)}, f32[32,256]{1,0:T(8,128)S(1)}, /*index=...) while((s32[]{:T(128)}, f32[8,256]{1,0:T(8,128)S(1)}, ...), condition=%wide.region_30.34_spmd, body=%wide.region_28.33_spmd.sunk | while | flops 70914864 | bytes 912737 | solution.py:106
  516.2 3.2 copy.51
  519.4 2.9 copy.54
  522.4 55.7 %while.75 = (s32[]{:T(128)}, f32[8,256,128]{2,1,0:T(8,128)}, f32[8,256]{1,0:T(8,128)S(1)}, pred[8,8]{1,0:T(8,128)(4,1)S(1)}, s32[8,8]{1,0:T(8,128)S(1)}, /*index...) while((s32[]{:T(128)}, f32[8,256,128]{2,1,0:T(8,128)}, ...), condition=%wide.region_33.37_spmd, body=%wide.region_31.36_spmd.sunk | while | flops 207492928 | bytes 5770245 | solution.py:122
  525.6 2.2 gather_fusion.16
  539.6 2.2 gather_fusion.16
  546.5 2.2 gather_fusion.16
  574.4 2.2 gather_fusion.16
  578.1 54.6 %pmax.39 = f32[2048]{0:T(1024)S(1)} all-reduce(f32[2048]{0:T(1024)S(1)} %bitcast.346), channel_id=1, replica_groups=mesh['src'=16,'tgt'=16] {'tgt'}, use_global_device_ids=true, to_apply=%region_34.38 | all-reduce | flops 2048 | bytes 16384 | tf_op jit(solution)/shard_map/pmax | solution.py:128
  632.8 2.6 bitcast_multiply_fusion
  635.4 27.6 %psum.47 = f32[2048]{0:T(1024)S(1)} all-reduce(f32[2048]{0:T(1024)S(1)} %get-tuple-element.646), channel_id=1, replica_groups=mesh['src'=16,'tgt'=16] {'tgt'}, use_global_device_ids=true, to_apply=%region_36.40 | all-reduce | flops 2048 | bytes 16384 | tf_op jit(solution)/shard_map/psum | solution.py:132
  663.1 90.1 %all-reduce.2.cloned.1.call-done = f32[2048,128]{1,0:T(8,128)} async-done(((f32[2048,128]{1,0:T(8,128)}), f32[2048,128]{1,0:T(8,128)}) %all-reduce.2.cloned.1.call-update) | async-done | bytes 1048592 | tf_op jit(solution)/shard_map/psum | solution.py:132
  (643 shorter events, 168.9 us)
Async XLA Ops:
  7.2 3.8 copy-start
  7.2 746.0 %all-reduce.2.cloned.1.call-start = ((), (), s32[]{:S(2)}) async-start(), calls=%async_computation | async-start | bytes 2097152 | tf_op jit(solution)/shard_map/psum | solution.py:132
  8.1 3.1 copy-start.6
  8.1 3.2 copy-start.3
  11.3 85.8 %copy-start.5 = (f32[2048]{0:T(1024)S(1)}, f32[2048]{0:T(1024)}, u32[]{:S(2)}) copy-start(f32[2048]{0:T(1024)} %param.28) | copy-start | bytes 24580
  97.1 145.1 %copy-start.2 = (f32[8192]{0:T(1024)S(1)}, f32[8192]{0:T(1024)}, u32[]{:S(2)}) copy-start(f32[8192]{0:T(1024)} %param.29) | copy-start | bytes 98308
  351.5 0.6 copy-start.4
  491.4 0.6 copy-start.1
Sparse Core Ops, SparseCore 0:
  635.5 117.6 all-reduce.1
where the time goes:
time: 762 us
  blocking collectives  467 us (61%)
  local copies, waits for them, and re-layouts  104 us (14%)
  waiting for transfers between devices  90.1 us (12%)
  matrix products  55.5 us (7%)
  other arithmetic  27.1 us (4%)
  between operations  14.5 us (2%)
    pmax x2, blocking collectives, merge_columns(): overall = lax.pmax(block_top, 'src')  126 us
    psum x2, blocking collectives, merge_columns(): return (overall, lax.psum(block_sum * jnp.exp(block_top - overall), 'src'))  117 us
    psum x1, waiting for transfers between devices, shards(): numerator, denominator = lax.psum((numerator, denominator), 'tgt')  90.1 us
    pmax x2, blocking collectives, merge_rows(): overall = lax.pmax(highest, 'tgt')  85.5 us
    psum x2, blocking collectives, merge_rows(): return (overall, lax.psum(totals * jnp.exp(highest - overall), 'tgt'))  56.9 us
    pmax x1, blocking collectives, shards(): overall = lax.pmax(local_top, 'tgt')  54.6 us
    dot_general x48, matrix products, pair_distance(): jnp.einsum('dr,dkc->krc', src_tile, tgt_chosen, preferred_element_type=jn...  45.6 us
    psum x1, blocking collectives, shards(): numerator, denominator = lax.psum((numerator, denominator), 'tgt')  27.6 us
  transfers between devices with their start and end apart: 1, of which 1 were waited for; matrix products, arithmetic and copies ran while one was open for 0% of the time, Pallas kernels for 0%

commit v1 on v0

--- a/solution.py
+++ b/solution.py
@@ -16,7 +16,7 @@
 
 def merge_rows(highest, totals):
     overall = lax.pmax(highest, "tgt")
-    return (overall, lax.psum(totals * jnp.exp(highest - overall), "tgt"))
+    return (overall, jnp.sum(lax.all_gather(totals * jnp.exp(highest - overall), "tgt"), axis=0))
 
 
 def merge_columns(block_top, block_sum):

time: 762 us -> 740 us (0.971)
  blocking collectives: 467 us -> 444 us
    psum x2 -> x0, blocking collectives: 56.9 us -> none  [merge_rows(): return (overall, lax.psum(totals * jnp.exp(highest - overall), 'tgt'))]
    all_gather x0 -> x2, blocking collectives: none -> 35.3 us  [merge_rows(): lax.all_gather(totals * jnp.exp(highest - overall), 'tgt')]
where the time goes in v1:
time: 740 us; the launch traced here: 739 us
  blocking collectives  444 us (60%)
  local copies, waits for them, and re-layouts  104 us (14%)
  waiting for transfers between devices  90 us (12%)
  matrix products  55.5 us (8%)
  other arithmetic  27.1 us (4%)
  between operations  14.5 us (2%)
    pmax x2, blocking collectives, merge_columns(): overall = lax.pmax(block_top, 'src')  125 us
    psum x2, blocking collectives, merge_columns(): return (overall, lax.psum(block_sum * jnp.exp(block_top - overall), 'src'))  117 us
    psum x1, waiting for transfers between devices, shards(): numerator, denominator = lax.psum((numerator, denominator), 'tgt')  90 us
    pmax x2, blocking collectives, merge_rows(): overall = lax.pmax(highest, 'tgt')  85.4 us
    pmax x1, blocking collectives, shards(): overall = lax.pmax(local_top, 'tgt')  54.6 us
    dot_general x48, matrix products, pair_distance(): jnp.einsum('dr,dkc->krc', src_tile, tgt_chosen, preferred_element_type=jn...  45.6 us
    all_gather x2, blocking collectives, merge_rows(): lax.all_gather(totals * jnp.exp(highest - overall), 'tgt')  35.3 us
    psum x1, blocking collectives, shards(): numerator, denominator = lax.psum((numerator, denominator), 'tgt')  27.6 us
  transfers between devices with their start and end apart: 1, of which 1 were waited for; matrix products, arithmetic and copies ran while one was open for 0% of the time, Pallas kernels for 0%

profile of v1, /device:TPU:1, one launch (start us, length us, event | category | flops | bytes accessed | tf_op | source)
XLA Modules:
  0.0 739.0 jit_solution(1789771213434570467)
XLA Ops:
  11.3 26.2 %while.70 = (s32[]{:T(128)}, f32[8,256]{1,0:T(8,128)S(1)}, f32[8,256]{1,0:T(8,128)S(1)}, pred[8,8]{1,0:T(8,128)(4,1)S(1)}, s32[8,8]{1,0:T(8,128)S(1)}, /*index=5...) while((s32[]{:T(128)}, f32[8,256]{1,0:T(8,128)S(1)}, ...), condition=%wide.region_5.8_spmd, body=%wide.region_2.7_spmd.sunk | while | flops 72487472 | bytes 5143929 | solution.py:76
  37.5 30.2 %pmax.35 = f32[2048]{0:T(1024)S(1)} all-reduce(f32[2048]{0:T(1024)S(1)} %bitcast.348), channel_id=1, replica_groups=mesh['src'=16,'tgt'=16] {'tgt'}, use_global_device_ids=true, to_apply=%region_6.9 | all-reduce | flops 2048 | bytes 16384 | tf_op jit(solution)/shard_map/pmax | solution.py:18
  67.8 18.5 %all-gather = f32[32768]{0:T(1024)S(1)} all-gather(f32[2048]{0:T(1024)S(1)} %exponential_multiply_fusion.3), channel_id=2, replica_groups=mesh['src'=16,'tgt'=16] {'tgt'}, dimensions={0}, use_global_device_ids=true | all-gather | bytes 139264 | tf_op jit(solution)/shard_map/all_gather | solution.py:19
  86.4 19.6 %while.71 = (s32[]{:T(128)}, f32[8,8,256]{2,1,0:T(8,128)S(1)}, f32[8,8,256]{2,1,0:T(8,128)S(1)}, pred[8,8]{1,0:T(8,128)(4,1)S(1)}, f32[8,256]{1,0:T(8,128)S(1)},...) while((s32[]{:T(128)}, f32[8,8,256]{2,1,0:T(8,128)S(1)}, ...), condition=%wide.region_11.14_spmd, body=%wide.region_8.13_spmd.sunk | while | flops 72481840 | bytes 5123405 | solution.py:91
  107.5 65.6 %pmax.36 = f32[8192]{0:T(1024)S(1)} all-reduce(f32[8192]{0:T(1024)S(1)} %bitcast.335), channel_id=1, replica_groups=mesh['src'=16,'tgt'=16] {'src'}, use_global_device_ids=true, to_apply=%region_13.16 | all-reduce | flops 8192 | bytes 65536 | tf_op jit(solution)/shard_map/pmax | solution.py:23
  173.1 58.0 %psum.28 = f32[8192]{0:T(1024)S(1)} all-reduce(f32[8192]{0:T(1024)S(1)} %exponential_multiply_fusion.1), channel_id=1, replica_groups=mesh['src'=16,'tgt'=16] {'src'}, use_global_device_ids=true, to_apply=%region_14.18 | all-reduce | flops 8192 | bytes 65536 | tf_op jit(solution)/shard_map/psum | solution.py:24
  231.2 26.1 %while.72 = (s32[]{:T(128)}, f32[8,256]{1,0:T(8,128)S(1)}, f32[8,256]{1,0:T(8,128)S(1)}, pred[8,8]{1,0:T(8,128)(4,1)S(1)}, s32[8,8]{1,0:T(8,128)S(1)}, /*index=5...) while((s32[]{:T(128)}, f32[8,256]{1,0:T(8,128)S(1)}, ...), condition=%wide.region_18.22_spmd, body=%wide.region_15.21_spmd.sunk | while | flops 72487472 | bytes 5111157 | solution.py:76
  257.4 55.2 %pmax.37 = f32[2048]{0:T(1024)S(1)} all-reduce(f32[2048]{0:T(1024)S(1)} %bitcast.350), channel_id=1, replica_groups=mesh['src'=16,'tgt'=16] {'tgt'}, use_global_device_ids=true, to_apply=%region_19.23 | all-reduce | flops 2048 | bytes 16384 | tf_op jit(solution)/shard_map/pmax | solution.py:18
  312.6 16.8 %all-gather.1 = f32[32768]{0:T(1024)S(1)} all-gather(f32[2048]{0:T(1024)S(1)} %exponential_multiply_fusion.2), channel_id=3, replica_groups=mesh['src'=16,'tgt'=16] {'tgt'}, dimensions={0}, use_global_device_ids=true | all-gather | bytes 139264 | tf_op jit(solution)/shard_map/all_gather | solution.py:19
  330.1 19.6 %while.73 = (s32[]{:T(128)}, f32[8,8,256]{2,1,0:T(8,128)S(1)}, f32[8,8,256]{2,1,0:T(8,128)S(1)}, pred[8,8]{1,0:T(8,128)(4,1)S(1)}, f32[8,256]{1,0:T(8,128)S(1)},...) while((s32[]{:T(128)}, f32[8,8,256]{2,1,0:T(8,128)S(1)}, ...), condition=%wide.region_24.28_spmd, body=%wide.region_21.27_spmd.sunk | while | flops 72481840 | bytes 5123405 | solution.py:91
  351.1 59.1 %pmax.38 = f32[8192]{0:T(1024)S(1)} all-reduce(f32[8192]{0:T(1024)S(1)} %bitcast.337), channel_id=1, replica_groups=mesh['src'=16,'tgt'=16] {'src'}, use_global_device_ids=true, to_apply=%region_26.30 | all-reduce | flops 8192 | bytes 65536 | tf_op jit(solution)/shard_map/pmax | solution.py:23
  410.3 58.6 %psum.29 = f32[8192]{0:T(1024)S(1)} all-reduce(f32[8192]{0:T(1024)S(1)} %exponential_multiply_fusion), channel_id=1, replica_groups=mesh['src'=16,'tgt'=16] {'src'}, use_global_device_ids=true, to_apply=%region_27.31 | all-reduce | flops 8192 | bytes 65536 | tf_op jit(solution)/shard_map/psum | solution.py:24
  469.5 24.2 %while.74 = (s32[]{:T(128)}, f32[8,256]{1,0:T(8,128)S(1)}, pred[8,8]{1,0:T(8,128)(4,1)S(1)}, s32[8,8]{1,0:T(8,128)S(1)}, f32[32,256]{1,0:T(8,128)S(1)}, /*index=...) while((s32[]{:T(128)}, f32[8,256]{1,0:T(8,128)S(1)}, ...), condition=%wide.region_30.34_spmd, body=%wide.region_28.33_spmd.sunk | while | flops 70914864 | bytes 912737 | solution.py:106
  493.7 3.2 copy.66
  496.9 2.9 copy.69
  499.9 55.7 %while.75 = (s32[]{:T(128)}, f32[8,256,128]{2,1,0:T(8,128)}, f32[8,256]{1,0:T(8,128)S(1)}, pred[8,8]{1,0:T(8,128)(4,1)S(1)}, s32[8,8]{1,0:T(8,128)S(1)}, /*index...) while((s32[]{:T(128)}, f32[8,256,128]{2,1,0:T(8,128)}, ...), condition=%wide.region_33.37_spmd, body=%wide.region_31.36_spmd.sunk | while | flops 207492928 | bytes 5770245 | solution.py:122
  510.1 2.2 gather_fusion.16
  524.0 2.2 gather_fusion.16
  531.0 2.2 gather_fusion.16
  538.0 2.2 gather_fusion.16
  555.6 54.6 %pmax.39 = f32[2048]{0:T(1024)S(1)} all-reduce(f32[2048]{0:T(1024)S(1)} %bitcast.346), channel_id=1, replica_groups=mesh['src'=16,'tgt'=16] {'tgt'}, use_global_device_ids=true, to_apply=%region_34.38 | all-reduce | flops 2048 | bytes 16384 | tf_op jit(solution)/shard_map/pmax | solution.py:128
  610.3 2.6 bitcast_multiply_fusion
  612.9 27.6 %psum.31 = f32[2048]{0:T(1024)S(1)} all-reduce(f32[2048]{0:T(1024)S(1)} %get-tuple-element.706), channel_id=1, replica_groups=mesh['src'=16,'tgt'=16] {'tgt'}, use_global_device_ids=true, to_apply=%region_36.40 | all-reduce | flops 2048 | bytes 16384 | tf_op jit(solution)/shard_map/psum | solution.py:132
  640.6 90.0 %all-reduce.2.cloned.1.call-done = f32[2048,128]{1,0:T(8,128)} async-done(((f32[2048,128]{1,0:T(8,128)}), f32[2048,128]{1,0:T(8,128)}) %all-reduce.2.cloned.1.call-update) | async-done | bytes 1048592 | tf_op jit(solution)/shard_map/psum | solution.py:132
  (647 shorter events, 169.1 us)
Async XLA Ops:
  7.2 3.8 copy-start
  7.2 723.4 %all-reduce.2.cloned.1.call-start = ((), (), s32[]{:S(2)}) async-start(), calls=%async_computation | async-start | bytes 2097152 | tf_op jit(solution)/shard_map/psum | solution.py:132
  8.1 3.1 copy-start.6
  8.1 3.2 copy-start.3
  11.3 75.0 %copy-start.5 = (f32[2048]{0:T(1024)S(1)}, f32[2048]{0:T(1024)}, u32[]{:S(2)}) copy-start(f32[2048]{0:T(1024)} %param.28) | copy-start | bytes 24580
  86.4 144.8 %copy-start.2 = (f32[8192]{0:T(1024)S(1)}, f32[8192]{0:T(1024)}, u32[]{:S(2)}) copy-start(f32[8192]{0:T(1024)} %param.29) | copy-start | bytes 98308
  329.5 0.6 copy-start.4
  468.9 0.6 copy-start.1
Sparse Core Ops, SparseCore 0:
  613.0 117.5 all-reduce.1
